TPU v7x, 32 devices: a whole 2x2x4 slice. The times are simulated.
32 devices in a mesh: coarse: 4 (over z), fine: 8 (over y, x, core).
Axes of the slice: x: 2, y: 2, z: 4, core: 2. Of those that a mesh axis runs over, the one named last changes fastest.
Arguments:
- right_side: float32 [64, 4096], P(None, ('coarse', 'fine')), may hold values from -6 to 6
- fine_diagonal: float32 [64, 64, 4096], P(None, None, ('coarse', 'fine'))
- fine_smoother: float32 [64, 64, 4096], P(None, None, ('coarse', 'fine'))
- fine_coupling: float32 [2, 64, 64, 4096], P(None, None, None, ('coarse', 'fine')), may hold values from -0.375 to 0.375
- fine_columns: int32 [2, 4096], P(None, ('coarse', 'fine')), may hold values from 0 to 191, as said below
- send_upward: int32 [1024], P(('coarse', 'fine')), may hold values from 0 to 127, as said below
- send_downward: int32 [1024], P(('coarse', 'fine')), may hold values from 0 to 127, as said below
- prolongation: float32 [64, 64, 4096], P(None, None, ('coarse', 'fine')), may hold values from -0.75 to 0.75
- aggregates: int32 [4096], P(('coarse', 'fine')), may hold values from 0 to 255, as said below
- coarse_diagonal: float32 [64, 64, 1024], P(None, None, ('coarse', 'fine'))
- coarse_smoother: float32 [64, 64, 1024], P(None, None, ('coarse', 'fine'))
- coarse_coupling: float32 [3, 64, 64, 1024], P(None, None, None, ('coarse', 'fine')), may hold values from -0.375 to 0.375
- coarse_columns: int32 [3, 1024], P(None, ('coarse', 'fine')), may hold values from 0 to 255, as said below
Outputs:
- fine_iterate: float32 [64, 4096], P(None, ('coarse', 'fine'))
- coarse_iterate: float32 [64, 1024], P(None, ('coarse', 'fine'))
Inputs may be any that keep to these rules, and one draw needn't show every extreme that they name: `fine_columns`: for block row n of device d: values below 32 name the blocks that device d - 1 lists in send_upward, in that order; values 32 to 159 name device d's own blocks in order; larger values name the blocks that device d + 1 lists in send_downward. No slot names the row's own block. Each of the 64 received blocks is named by slot 0 of at least one row of the device. `send_upward`: 32 distinct local block numbers for each device. `send_downward`: 32 distinct local block numbers for each device. aggregates: numbered within the coarse group as f * 32 + j for the j-th coarse block of the group's device f along fine. Every aggregate holds exactly 4 fine blocks, and the blocks of each device name the aggregates of each device of its coarse group exactly 16 times. coarse_columns: numbered within the coarse group as for aggregates; never the row's own block. Among the 96 entries of one device's rows, at most 12 name blocks of any one device of the group, and some device's blocks are named exactly 12 times.
All inputs are finite; a program needn't handle non-finite values.
Results may differ from a plain program's by a relative error of at most 0.0003.
Values sent between devices are 32-bit elements; how exact they have to be, the bound alone decides.
A program may use at most 64 MiB of HBM per device.

v0:
```python
import jax
import jax.numpy as jnp
from jax import lax
from jax.sharding import PartitionSpec as P

FINE_SWEEPS = 3
COARSE_SWEEPS = 5


def from_behind(value, axis, steps):
    count = lax.axis_size(axis)
    leading, last = (max(0, -steps), min(count, count - steps))
    return lax.ppermute(value, axis, [(source, source + steps) for source in range(leading, last)])


def apply_blocks(blocks, vector):
    return jnp.einsum("abn,bn->an", blocks, vector, precision=lax.Precision.HIGHEST)


def apply_transposed(blocks, vector):
    return jnp.einsum("abn,an->bn", blocks, vector, precision=lax.Precision.HIGHEST)


def fine_operator(values, fine_diagonal, fine_coupling, fine_columns, send_upward, send_downward):
    upward = values[:, send_upward]
    downward = values[:, send_downward]
    lower_rim = from_behind(upward, ("coarse", "fine"), 1)
    upper_rim = from_behind(downward, ("coarse", "fine"), -1)
    summed = apply_blocks(fine_diagonal, values)
    extended = jnp.concatenate([lower_rim, values, upper_rim], axis=1)
    for neighbour in range(fine_coupling.shape[0]):
        summed = summed + apply_blocks(
            fine_coupling[neighbour], extended[:, fine_columns[neighbour]]
        )
    return summed


def body(
    right_side,
    fine_diagonal,
    fine_smoother,
    fine_coupling,
    fine_columns,
    send_upward,
    send_downward,
    prolongation,
    aggregates,
    coarse_diagonal,
    coarse_smoother,
    coarse_coupling,
    coarse_columns,
):
    iterate = apply_blocks(fine_smoother, right_side)
    for sweep_num in range(FINE_SWEEPS - 1):
        image = fine_operator(
            iterate, fine_diagonal, fine_coupling, fine_columns, send_upward, send_downward
        )
        iterate = iterate + apply_blocks(fine_smoother, right_side - image)
    residual = right_side - fine_operator(
        iterate, fine_diagonal, fine_coupling, fine_columns, send_upward, send_downward
    )
    pulled = apply_transposed(prolongation, residual)
    coarse_count = coarse_diagonal.shape[2]
    targets = jnp.arange(coarse_count * lax.axis_size("fine"), dtype=jnp.int32)
    onehot = (aggregates[:, None] == targets[None, :]).astype(jnp.float32)
    coarse_rhs = lax.psum_scatter(
        jnp.dot(pulled, onehot, precision=lax.Precision.HIGHEST).T,
        "fine",
        scatter_dimension=0,
        tiled=True,
    ).T
    neighbours = coarse_coupling.shape[0]
    correction = apply_blocks(coarse_smoother, coarse_rhs)
    for sweep_num in range(COARSE_SWEEPS - 1):
        image = apply_blocks(coarse_diagonal, correction)
        gathered = lax.all_gather(correction, "fine", axis=1, tiled=True)
        for neighbour in range(neighbours):
            image = image + apply_blocks(
                coarse_coupling[neighbour], gathered[:, coarse_columns[neighbour]]
            )
        correction = correction + apply_blocks(coarse_smoother, coarse_rhs - image)
    return (iterate, correction)


def solution(mesh):
    in_specs = (
        P(None, ("coarse", "fine")),
        P(None, None, ("coarse", "fine")),
        P(None, None, ("coarse", "fine")),
        P(None, None, None, ("coarse", "fine")),
        P(None, ("coarse", "fine")),
        P(("coarse", "fine")),
        P(("coarse", "fine")),
        P(None, None, ("coarse", "fine")),
        P(("coarse", "fine")),
        P(None, None, ("coarse", "fine")),
        P(None, None, ("coarse", "fine")),
        P(None, None, None, ("coarse", "fine")),
        P(None, ("coarse", "fine")),
    )
    out_specs = (P(None, ("coarse", "fine")), P(None, ("coarse", "fine")))
    return jax.shard_map(body, mesh=mesh, in_specs=in_specs, out_specs=out_specs, check_vma=False)
```

profile of v0, /device:TPU:0, one launch (start us, length us, event | category | flops | bytes accessed | tf_op | source)
XLA Modules:
  0.0 183.4 jit_solution(2015682138323736880)
XLA Ops:
  7.3 2.1 %multiply_reduce_fusion.6 = f32[128,64]{0,1:T(8,128)S(1)} fusion(f32[64,64,128]{2,1,0:T(8,128)} %param.15, f32[128,64]{0,1:T(8,128)} %bitcast.328), kind=kLoop, calls=%fused_computation.42 | loop fusion | flops 1040384 | bytes 2162688
  10.0 2.4 %collective-permute-start = (f32[64,32]{0,1:T(8,128)S(1)}, f32[64,32]{0,1:T(8,128)S(1)}, u32[]{:S(2)}, u32[]{:S(2)}) collective-permute-start(f32[64,32]{0,1:T(8,128)S(1)} %bitcast.371), channel_id=1, source_target_pairs={{0,1},{1,2},{2,3},{3,4},{4,5},{5,6},{6,7},{7,8},{8,9},{9,10},{10,1... | collective-permute-start | bytes 24584 | tf_op jit(solution)/shard_map/ppermute | solution.py:13
  14.7 3.6 %slice_bitcast_fusion.2 = (f32[64,64,32]{1,2,0:T(8,128)}, f32[64,64,32]{1,2,0:T(8,128)}, f32[64,64,32]{1,2,0:T(8,128)S(1)}) fusion(f32[3,64,64,32]{2,3,1,0:T(8,128)} %param.24), kind=kLoop, calls=%fused_computation.45 | loop fusion | bytes 3145728 | tf_op jit(solution)/shard_map/squeeze | solution.py:79
  21.4 2.8 %copy.115 = f32[64,64,32]{0,1,2:T(8,128)} copy(f32[64,64,32]{1,2,0:T(8,128)} %get-tuple-element.10) | data formatting | bytes 1048576 | tf_op jit(solution)/shard_map/squeeze | solution.py:79
  24.1 2.8 %copy.112 = f32[64,64,32]{0,1,2:T(8,128)} copy(f32[64,64,32]{1,2,0:T(8,128)} %param.22) | data formatting | bytes 1048576 | tf_op args[9]
  28.4 3.1 %fusion.3 = (f32[128,64]{0,1:T(8,128)S(1)}, f32[128,64]{0,1:T(8,128)S(1)}) fusion(f32[2,64,64,128]{3,2,1,0:T(8,128)} %param.16, f32[128,64]{0,1:T(8,128)S(1)} %copy.158, f32[128,64]{0,1:T(8,128)S(1)} %copy.159), kind=kLoop, calls=%fused_computation.33 | loop fusion | flops 2080768 | bytes 4325376 | tf_op jit(solution)/shard_map/abn,bn->an/dot_general | solution.py:17
  33.2 5.1 %collective-permute-start.2 = (f32[64,32]{0,1:T(8,128)S(1)}, f32[64,32]{0,1:T(8,128)S(1)}, u32[]{:S(2)}, u32[]{:S(2)}) collective-permute-start(f32[64,32]{0,1:T(8,128)S(1)} %bitcast.376), channel_id=1, source_target_pairs={{0,1},{1,2},{2,3},{3,4},{4,5},{5,6},{6,7},{7,8},{8,9},{9,10},{10,1... | collective-permute-start | bytes 24584 | tf_op jit(solution)/shard_map/ppermute | solution.py:13
  39.7 1.9 %multiply_reduce_fusion.3 = f32[128,64]{0,1:T(8,128)S(1)} fusion(f32[64,64,128]{2,1,0:T(8,128)} %param.14, f32[128,64]{0,1:T(8,128)S(1)} %copy.161), kind=kLoop, calls=%fused_computation.39 | loop fusion | flops 1040384 | bytes 2162688 | tf_op jit(solution)/shard_map/abn,bn->an/dot_general | solution.py:17
  44.1 3.1 %fusion.4 = (f32[128,64]{0,1:T(8,128)S(1)}, f32[128,64]{0,1:T(8,128)S(1)}) fusion(f32[2,64,64,128]{3,2,1,0:T(8,128)} %param.16, f32[128,64]{0,1:T(8,128)S(1)} %copy.162, f32[128,64]{0,1:T(8,128)S(1)} %copy.163), kind=kLoop, calls=%fused_computation.34 | loop fusion | flops 2080768 | bytes 4325376 | tf_op jit(solution)/shard_map/abn,bn->an/dot_general | solution.py:17
  48.9 4.4 %collective-permute-start.4 = (f32[64,32]{0,1:T(8,128)S(1)}, f32[64,32]{0,1:T(8,128)S(1)}, u32[]{:S(2)}, u32[]{:S(2)}) collective-permute-start(f32[64,32]{0,1:T(8,128)S(1)} %bitcast.375), channel_id=1, source_target_pairs={{0,1},{1,2},{2,3},{3,4},{4,5},{5,6},{6,7},{7,8},{8,9},{9,10},{10,1... | collective-permute-start | bytes 24584 | tf_op jit(solution)/shard_map/ppermute | solution.py:13
  54.6 1.9 %multiply_reduce_fusion.1 = f32[128,64]{0,1:T(8,128)S(1)} fusion(f32[64,64,128]{2,1,0:T(8,128)} %param.14, f32[128,64]{0,1:T(8,128)S(1)} %copy.165), kind=kLoop, calls=%fused_computation.37 | loop fusion | flops 1040384 | bytes 2162688 | tf_op jit(solution)/shard_map/abn,bn->an/dot_general | solution.py:17
  58.1 3.1 %fusion.5 = (f32[128,64]{0,1:T(8,128)S(1)}, f32[128,64]{0,1:T(8,128)S(1)}) fusion(f32[2,64,64,128]{3,2,1,0:T(8,128)} %param.16, f32[128,64]{0,1:T(8,128)S(1)} %copy.166, f32[128,64]{0,1:T(8,128)S(1)} %copy.167), kind=kLoop, calls=%fused_computation.35 | loop fusion | flops 2080768 | bytes 4325376 | tf_op jit(solution)/shard_map/abn,bn->an/dot_general | solution.py:17
  63.6 40.4 %reduce-scatter.2.cloned.1.call-done = f32[32,64]{1,0:T(8,128)} async-done(((f32[256,64]{1,0:T(8,128)}), f32[32,64]{1,0:T(8,128)}) %reduce-scatter.2.cloned.1.call-update) | async-done | bytes 8208 | tf_op jit(solution)/shard_map/reduce_scatter | solution.py:66
  105.7 9.4 %all_gather.12 = f32[64,256]{0,1:T(8,128)S(1)} all-gather(f32[64,32]{0,1:T(8,128)S(1)} %bitcast.330), channel_id=1, replica_groups=mesh['coarse'=4,'fine'=8] {'fine'}, dimensions={1}, use_global_device_ids=true | all-gather | bytes 73728 | tf_op jit(solution)/shard_map/all_gather | solution.py:76
  116.8 2.3 %fusion.13 = f32[32,1,64]{2,1,0:T(1,128)S(1)} fusion(f32[64,64,32]{0,1,2:T(8,128)} %copy.112, f32[32,1,64]{2,1,0:T(1,128)S(1)} %fusion.20), kind=kOutput, calls=%fused_computation.61 | convolution fusion | flops 1572864 | bytes 540672 | tf_op jit(solution)/shard_map/abn,bn->an/dot_general | solution.py:17
  123.0 8.2 %all_gather.13 = f32[64,256]{0,1:T(8,128)S(1)} all-gather(f32[64,32]{0,1:T(8,128)S(1)} %add.201), channel_id=1, replica_groups=mesh['coarse'=4,'fine'=8] {'fine'}, dimensions={1}, use_global_device_ids=true | all-gather | bytes 73728 | tf_op jit(solution)/shard_map/all_gather | solution.py:76
  132.9 2.2 %fusion.26 = f32[32,1,64]{2,1,0:T(1,128)S(1)} fusion(f32[64,32,1]{0,2,1:T(1,128)S(1)} %bitcast.345, f32[64,64,32]{0,1,2:T(8,128)} %copy.115), kind=kOutput, calls=%fused_computation.92 | convolution fusion | flops 1572864 | bytes 540672 | tf_op jit(solution)/shard_map/abn,bn->an/dot_general | solution.py:17
  135.1 2.2 %fusion.25 = f32[32,1,64]{2,1,0:T(1,128)S(1)} fusion(f32[64,32,1]{0,2,1:T(1,128)S(1)} %bitcast.333, f32[64,64,32]{0,1,2:T(8,128)} %copy.112), kind=kOutput, calls=%fused_computation.91 | convolution fusion | flops 1572864 | bytes 540672 | tf_op jit(solution)/shard_map/abn,bn->an/dot_general | solution.py:17
  140.2 9.4 %all_gather.14 = f32[64,256]{0,1:T(8,128)S(1)} all-gather(f32[64,32]{0,1:T(8,128)S(1)} %add.206), channel_id=1, replica_groups=mesh['coarse'=4,'fine'=8] {'fine'}, dimensions={1}, use_global_device_ids=true | all-gather | bytes 73728 | tf_op jit(solution)/shard_map/all_gather | solution.py:76
  151.4 2.2 %fusion.31 = f32[32,1,64]{2,1,0:T(1,128)S(1)} fusion(f32[64,32,1]{0,2,1:T(1,128)S(1)} %bitcast.346, f32[64,64,32]{0,1,2:T(8,128)} %copy.115), kind=kOutput, calls=%fused_computation.97 | convolution fusion | flops 1572864 | bytes 540672 | tf_op jit(solution)/shard_map/abn,bn->an/dot_general | solution.py:17
  153.5 2.2 %fusion.30 = f32[32,1,64]{2,1,0:T(1,128)S(1)} fusion(f32[64,32,1]{0,2,1:T(1,128)S(1)} %bitcast.334, f32[64,64,32]{0,1,2:T(8,128)} %copy.112), kind=kOutput, calls=%fused_computation.96 | convolution fusion | flops 1572864 | bytes 540672 | tf_op jit(solution)/shard_map/abn,bn->an/dot_general | solution.py:17
  158.7 8.2 %all_gather.15 = f32[64,256]{0,1:T(8,128)S(1)} all-gather(f32[64,32]{0,1:T(8,128)S(1)} %add.211), channel_id=1, replica_groups=mesh['coarse'=4,'fine'=8] {'fine'}, dimensions={1}, use_global_device_ids=true | all-gather | bytes 73728 | tf_op jit(solution)/shard_map/all_gather | solution.py:76
  168.6 2.2 %fusion.36 = f32[32,1,64]{2,1,0:T(1,128)S(1)} fusion(f32[64,32,1]{0,2,1:T(1,128)S(1)} %bitcast.337, f32[64,64,32]{0,1,2:T(8,128)} %copy.115), kind=kOutput, calls=%fused_computation.102 | convolution fusion | flops 1572864 | bytes 540672 | tf_op jit(solution)/shard_map/abn,bn->an/dot_general | solution.py:17
  170.8 2.2 %fusion.35 = f32[32,1,64]{2,1,0:T(1,128)S(1)} fusion(f32[64,32,1]{0,2,1:T(1,128)S(1)} %bitcast.332, f32[64,64,32]{0,1,2:T(8,128)} %copy.112), kind=kOutput, calls=%fused_computation.101 | convolution fusion | flops 1572864 | bytes 540672 | tf_op jit(solution)/shard_map/abn,bn->an/dot_general | solution.py:17
  (120 shorter events, 41.5 us)
Async XLA Ops:
  7.2 2.3 %copy-start.11 = (s32[32]{0:T(128)S(1)}, s32[32]{0:T(128)}, u32[]{:S(2)}) copy-start(s32[32]{0:T(128)} %param.18) | copy-start | bytes 388
  7.2 5.2 %copy-start.12 = (s32[32]{0:T(128)S(1)}, s32[32]{0:T(128)}, u32[]{:S(2)}) copy-start(s32[32]{0:T(128)} %param.19) | copy-start | bytes 388
  7.2 7.1 %copy-start.9 = (s32[2,128]{1,0:T(2,128)S(1)}, s32[2,128]{1,0:T(2,128)}, u32[]{:S(2)}) copy-start(s32[2,128]{1,0:T(2,128)} %param.17) | copy-start | bytes 3076
  7.2 7.1 %copy-start.3 = (f32[64,64,128]{2,1,0:T(8,128)S(1)}, f32[64,64,128]{2,1,0:T(8,128)}, u32[]{:S(2)}) copy-start(f32[64,64,128]{2,1,0:T(8,128)} %param.14) | copy-start | bytes 6291460
  7.2 96.8 %reduce-scatter.2.cloned.1.call-start = ((), (), s32[]{:S(2)}) async-start(), calls=%async_computation.1 | async-start | bytes 147456 | tf_op jit(solution)/shard_map/reduce_scatter | solution.py:66
  7.3 7.4 %copy-start.8 = (s32[3,32]{1,0:T(4,128)S(1)}, s32[3,32]{1,0:T(4,128)}, u32[]{:S(2)}) copy-start(s32[3,32]{1,0:T(4,128)} %param.25) | copy-start | bytes 1156
  10.0 16.9 %collective-permute-start = (f32[64,32]{0,1:T(8,128)S(1)}, f32[64,32]{0,1:T(8,128)S(1)}, u32[]{:S(2)}, u32[]{:S(2)}) collective-permute-start(f32[64,32]{0,1:T(8,128)S(1)} %bitcast.371), channel_id=1, source_target_pairs={{0,1},{1,2},{2,3},{3,4},{4,5},{5,6},{6,7},{7,8},{8,9},{9,10},{10,1... | collective-permute-start | bytes 24584 | tf_op jit(solution)/shard_map/ppermute | solution.py:13
  13.0 13.9 %collective-permute-start.1 = (f32[64,32]{0,1:T(8,128)S(1)}, f32[64,32]{0,1:T(8,128)S(1)}, u32[]{:S(2)}, u32[]{:S(2)}) collective-permute-start(f32[64,32]{0,1:T(8,128)S(1)} %bitcast.372), channel_id=1, source_target_pairs={{1,0},{2,1},{3,2},{4,3},{5,4},{6,5},{7,6},{8,7},{9,8},{10,9},{11,1... | collective-permute-start | bytes 24584 | tf_op jit(solution)/shard_map/ppermute | solution.py:13
  14.7 3.6 %copy-start.5 = (f32[64,64,32]{1,2,0:T(8,128)S(1)}, f32[64,64,32]{1,2,0:T(8,128)}, u32[]{:S(2)}) copy-start(f32[64,64,32]{1,2,0:T(8,128)} %param.23) | copy-start | bytes 1572868
  28.4 3.2 %copy-start.6 = (f32[64,128]{1,0:T(8,128)S(1)}, f32[64,128]{1,0:T(8,128)}, u32[]{:S(2)}) copy-start(f32[64,128]{1,0:T(8,128)} %param.13) | copy-start | bytes 98308
  28.4 3.2 %copy-start.1 = (f32[64,64,128]{2,1,0:T(8,128)S(1)}, f32[64,64,128]{2,1,0:T(8,128)}, u32[]{:S(2)}) copy-start(f32[64,64,128]{2,1,0:T(8,128)} %param.15) | copy-start | bytes 6291460
  33.2 8.5 %collective-permute-start.2 = (f32[64,32]{0,1:T(8,128)S(1)}, f32[64,32]{0,1:T(8,128)S(1)}, u32[]{:S(2)}, u32[]{:S(2)}) collective-permute-start(f32[64,32]{0,1:T(8,128)S(1)} %bitcast.376), channel_id=1, source_target_pairs={{0,1},{1,2},{2,3},{3,4},{4,5},{5,6},{6,7},{7,8},{8,9},{9,10},{10,1... | collective-permute-start | bytes 24584 | tf_op jit(solution)/shard_map/ppermute | solution.py:13
  38.4 4.3 %collective-permute-start.3 = (f32[64,32]{0,1:T(8,128)S(1)}, f32[64,32]{0,1:T(8,128)S(1)}, u32[]{:S(2)}, u32[]{:S(2)}) collective-permute-start(f32[64,32]{0,1:T(8,128)S(1)} %bitcast.374), channel_id=1, source_target_pairs={{1,0},{2,1},{3,2},{4,3},{5,4},{6,5},{7,6},{8,7},{9,8},{10,9},{11,1... | collective-permute-start | bytes 24584 | tf_op jit(solution)/shard_map/ppermute | solution.py:13
  44.1 3.2 %copy-start.2 = (f32[64,64,128]{2,1,0:T(8,128)S(1)}, f32[64,64,128]{2,1,0:T(8,128)}, u32[]{:S(2)}) copy-start(f32[64,64,128]{2,1,0:T(8,128)} %param.15) | copy-start | bytes 6291460
  48.9 7.7 %collective-permute-start.4 = (f32[64,32]{0,1:T(8,128)S(1)}, f32[64,32]{0,1:T(8,128)S(1)}, u32[]{:S(2)}, u32[]{:S(2)}) collective-permute-start(f32[64,32]{0,1:T(8,128)S(1)} %bitcast.375), channel_id=1, source_target_pairs={{0,1},{1,2},{2,3},{3,4},{4,5},{5,6},{6,7},{7,8},{8,9},{9,10},{10,1... | collective-permute-start | bytes 24584 | tf_op jit(solution)/shard_map/ppermute | solution.py:13
  53.3 3.3 %collective-permute-start.5 = (f32[64,32]{0,1:T(8,128)S(1)}, f32[64,32]{0,1:T(8,128)S(1)}, u32[]{:S(2)}, u32[]{:S(2)}) collective-permute-start(f32[64,32]{0,1:T(8,128)S(1)} %bitcast.373), channel_id=1, source_target_pairs={{1,0},{2,1},{3,2},{4,3},{5,4},{6,5},{7,6},{8,7},{9,8},{10,9},{11,1... | collective-permute-start | bytes 24584 | tf_op jit(solution)/shard_map/ppermute | solution.py:13
  58.1 3.2 %copy-start.4 = (f32[64,64,128]{2,1,0:T(8,128)S(1)}, f32[64,64,128]{2,1,0:T(8,128)}, u32[]{:S(2)}) copy-start(f32[64,64,128]{2,1,0:T(8,128)} %param.20) | copy-start | bytes 6291460
  61.2 0.7 copy-start.10
  116.8 4.2 %copy-start = (f32[64,64,32]{0,1,2:T(8,128)S(1)}, f32[64,64,32]{0,1,2:T(8,128)}, u32[]{:S(2)}) copy-start(f32[64,64,32]{0,1,2:T(8,128)} %copy.115) | copy-start | bytes 1572868
  116.8 5.2 %copy-start.7 = (f32[32,64]{1,0:T(8,128)S(1)}, f32[32,64]{1,0:T(8,128)}, u32[]{:S(2)}) copy-start(f32[32,64]{1,0:T(8,128)} %reduce-scatter.2.cloned.1.call-done) | copy-start | bytes 24580
Sparse Core Ops, SparseCore 0:
  63.0 40.9 reduce-scatter.1
where the time goes:
time: 184 us; the launch traced here: 183 us
  waiting for transfers between devices  41.4 us (22%)
  blocking collectives  35.3 us (19%)
  matrix products  30.6 us (17%)
  local copies, waits for them, and re-layouts  28.3 us (15%)
  other arithmetic  17.4 us (9%)
  starting transfers between devices  15.8 us (9%)
  between operations  14.5 us (8%)
    reduce_scatter x1, waiting for transfers between devices, body(): lax.psum_scatter(jnp.dot(pulled, onehot, precision=lax.Precision.HIGHEST)...  40.4 us
    all_gather x4, blocking collectives, body(): gathered = lax.all_gather(correction, 'fine', axis=1, tiled=True)  35.3 us
    dot_general x21, matrix products, apply_blocks(): jnp.einsum('abn,bn->an', blocks, vector, precision=lax.Precision.HIGHEST)  29.6 us
    ppermute x6, starting transfers between devices, from_behind(): lax.ppermute(value, axis, [(source, source + steps) for source in range(l...  15.7 us
    dot_general x6, other arithmetic, apply_blocks(): jnp.einsum('abn,bn->an', blocks, vector, precision=lax.Precision.HIGHEST)  13.6 us
    squeeze x4, local copies, waits for them, and re-layouts, body(): coarse_coupling[neighbour]  8.77 us
    gather x12, local copies, waits for them, and re-layouts, body(): gathered[:, coarse_columns[neighbour]]  6.87 us
    unnamed x37, local copies, waits for them, and re-layouts  5.1 us
  transfers between devices with their start and end apart: 7, of which 2 were waited for; matrix products, arithmetic and copies ran while one was open for 10% of the time, Pallas kernels for 0%

commit v1 on v0

v1 whole, which is shorter than its diff:
```python
import functools

import jax
import jax.numpy as jnp
from jax import lax
from jax.experimental import pallas as pl
from jax.experimental.pallas import tpu as pltpu
from jax.sharding import PartitionSpec as P

FINE_SWEEPS = 3
COARSE_SWEEPS = 5
MESH = pl.DeviceIdType.MESH
LANES = 128
SUB = 8


def lane_gather(values, index):
    return jnp.take_along_axis(values, index, axis=1)


def sublane_sums(parts):
    row = lax.broadcasted_iota(jnp.int32, (SUB, LANES), 0)
    for bit in (1, 2, 4):
        keep = (row & bit) == 0
        parts = [
            jnp.where(keep, x, y) + pltpu.roll(jnp.where(keep, y, x), SUB - bit, 0)
            for x, y in zip(parts[0::2], parts[1::2])
        ]
    return parts[0]


def product_rows(blocks, vectors, base):
    sums = []
    for a in range(SUB):
        total = None
        for block, vector in zip(blocks, vectors):
            value = block[base + a]
            for s in range(0, value.shape[0], SUB):
                term = value[s : s + SUB] * vector[s : s + SUB]
                total = term if total is None else total + term
        sums.append(total)
    return sublane_sums(sums)


def loop_rows(count, unroll, body):
    def step(i, carry):
        body(pl.multiple_of(i * SUB, SUB))
        return carry

    lax.fori_loop(0, count // SUB, step, 0, unroll=unroll)


def kernel(
    n_coarse, n_fine,
    rs, fd, fs, fc, fcol, su, sd, pr, ag, cd, cs, cc, ccol,
    x_out, y_out,
    rs_v, fd_v, fs_v, fc_v, pr_v, cd_v, cs_v, cc_v,
    packed_op, packed_sm, x_v, ax_v, lower, upper, send_up, send_down,
    onehot, restricted, part_send, part_recv, gathered, gather4, index_v,
    load_sem, chain_send, chain_recv, part_ssem, part_rsem, y_ssem, y_rsem,
):
    c, f = lax.axis_index("coarse"), lax.axis_index("fine")
    node = rs.shape[0]
    groups = LANES // ccol.shape[1]
    width = ccol.shape[1]
    tall = node // groups
    loads = []
    for slot, (src, dst) in enumerate(
        [(rs, rs_v), (fs, fs_v), (fd, fd_v), (fc, fc_v), (pr, pr_v), (cc, cc_v), (cd, cd_v), (cs, cs_v)]
    ):
        load = pltpu.make_async_copy(src, dst, load_sem.at[slot])
        load.start()
        loads.append(load)

    has_lower = jnp.logical_or(c > 0, f > 0)
    has_upper = jnp.logical_or(c < n_coarse - 1, f < n_fine - 1)
    down_id = (jnp.where(f > 0, c, c - 1), jnp.where(f > 0, f - 1, n_fine - 1))
    up_id = (jnp.where(f < n_fine - 1, c, c + 1), jnp.where(f < n_fine - 1, f + 1, 0))

    def peer(t):
        return (c, lax.rem(f + t, n_fine))

    barrier = pltpu.get_barrier_semaphore()

    def greet(t, carry):
        pl.semaphore_signal(barrier, inc=1, device_id=peer(t), device_id_type=MESH)
        return carry

    lax.fori_loop(1, n_fine, greet, 0)
    cross_down = jnp.logical_and(f == 0, c > 0)
    cross_up = jnp.logical_and(f == n_fine - 1, c < n_coarse - 1)

    @pl.when(cross_down)
    def _():
        pl.semaphore_signal(barrier, inc=1, device_id=down_id, device_id_type=MESH)

    @pl.when(cross_up)
    def _():
        pl.semaphore_signal(barrier, inc=1, device_id=up_id, device_id_type=MESH)

    lane16 = lax.broadcasted_iota(jnp.int32, (SUB, LANES), 1)
    lane_group = lane16 // width
    lane_mod = lane16 % width

    index_v[...] = jnp.zeros_like(index_v)
    index_v[0:1, 0:width] = su[...]
    index_v[SUB : SUB + 1, 0:width] = sd[...]
    for k in range(groups - 1):
        index_v[(2 + k) * SUB : (2 + k) * SUB + 1, 0:width] = ccol[k : k + 1, :]

    def spread(k):
        row = jnp.broadcast_to(index_v[k * SUB : k * SUB + 1, :], (SUB, LANES))
        return lane_gather(row, lane_mod)

    up_index, down_index = spread(0), spread(1)
    rim = width
    wanted = f * width + lane_mod
    for k in range(groups - 1):
        wanted = jnp.where(lane_group == k, spread(2 + k), wanted)
    wanted_slot = lax.rem(f - wanted // width + n_fine, n_fine)
    wanted_lane = lax.rem(wanted, width)

    agg = ag[...]
    agg_slot = lax.rem(agg // width - f + n_fine, n_fine) * width + lax.rem(agg, width)

    def hot_rows(t, carry):
        base = pl.multiple_of(t * width, width)
        target = base + lax.broadcasted_iota(jnp.int32, (width, LANES), 0)
        onehot[pl.ds(base, width), :] = (target == agg_slot).astype(jnp.float32).astype(jnp.bfloat16)
        return carry

    lax.fori_loop(0, n_fine, hot_rows, 0)

    @pl.when(jnp.logical_not(has_lower))
    def _():
        lower[...] = jnp.zeros_like(lower)

    @pl.when(jnp.logical_not(has_upper))
    def _():
        upper[...] = jnp.zeros_like(upper)

    loads[0].wait()
    right = rs_v[...]
    loads[1].wait()

    def first_rows(base):
        x_v[pl.ds(base, SUB), :] = product_rows([fs_v], [right], base)

    loop_rows(node, 1, first_rows)

    pl.semaphore_wait(barrier, n_fine - 1 + cross_down.astype(jnp.int32) + cross_up.astype(jnp.int32))

    def up_copy(s):
        return pltpu.make_async_remote_copy(
            send_up.at[s], lower.at[s], chain_send.at[0, s], chain_recv.at[0, s], device_id=up_id, device_id_type=MESH
        )

    def down_copy(s):
        return pltpu.make_async_remote_copy(
            send_down.at[s], upper.at[s], chain_send.at[1, s], chain_recv.at[1, s], device_id=down_id, device_id_type=MESH
        )

    def pack_rows(values, index):
        out = []
        for h in range(0, tall, SUB):
            total = None
            for g in range(groups):
                piece = lane_gather(values[g * tall + h : g * tall + h + SUB], index)
                total = piece if total is None else jnp.where(lane_group == g, piece, total)
            out.append(total)
        return jnp.concatenate(out, axis=0)

    columns = [jnp.broadcast_to(fcol[k : k + 1, :], (SUB, LANES)) for k in range(fcol.shape[0])]
    local = [jnp.clip(col - rim, 0, LANES - 1) for col in columns]
    low = [jnp.clip(col, 0, rim - 1) for col in columns]
    high = [jnp.clip(col - rim - LANES, 0, rim - 1) for col in columns]
    is_low = [col < rim for col in columns]
    is_high = [col >= rim + LANES for col in columns]

    def pack_coarse(part, parts):
        def op_row(a, carry):
            packed_op[a] = jnp.concatenate([cc_v[k, a] for k in range(groups - 1)] + [cd_v[a]], axis=0).T
            return carry

        def sm_row(a, carry):
            packed_sm[a] = jnp.concatenate([cs_v[g * tall + a] for g in range(groups)], axis=0).T
            return carry

        lax.fori_loop(part * node // parts, (part + 1) * node // parts, op_row, 0)
        lax.fori_loop(part * tall // parts, (part + 1) * tall // parts, sm_row, 0)

    parts = 2
    for s in range(FINE_SWEEPS):
        x = x_v[...]
        send_up[s] = pack_rows(x, up_index)
        send_down[s] = pack_rows(x, down_index)

        @pl.when(has_upper)
        def _():
            up_copy(s).start()

        @pl.when(has_lower)
        def _():
            down_copy(s).start()

        if s == 0:
            loads[2].wait()

        def diag_rows(base):
            ax_v[pl.ds(base, SUB), :] = product_rows([fd_v], [x], base)

        loop_rows(node, 1, diag_rows)
        if s == 0:
            loads[3].wait()
        if s == 1:
            for load in loads[5:]:
                load.wait()
        if s >= 1:
            pack_coarse(s - 1, parts)

        @pl.when(has_lower)
        def _():
            up_copy(s).wait_recv()

        @pl.when(has_upper)
        def _():
            down_copy(s).wait_recv()

        picked = []
        for k in range(len(columns)):
            rows = []
            for v in range(node // SUB):
                g, h = v * SUB // tall, v * SUB % tall
                own = lane_gather(x[v * SUB : v * SUB + SUB], local[k])
                below = lane_gather(lower[s, h : h + SUB], low[k] + g * width)
                above = lane_gather(upper[s, h : h + SUB], high[k] + g * width)
                rows.append(jnp.where(is_low[k], below, jnp.where(is_high[k], above, own)))
            picked.append(jnp.concatenate(rows, axis=0))

        def coupling_rows(base):
            at = pl.ds(base, SUB)
            image = product_rows([fc_v.at[k] for k in range(len(columns))], picked, base)
            ax_v[at, :] = rs_v[at, :] - (ax_v[at, :] + image)

        loop_rows(node, 1, coupling_rows)
        if s < FINE_SWEEPS - 1:
            res = ax_v[...]

            def smooth_rows(base):
                at = pl.ds(base, SUB)
                x_v[at, :] = x_v[at, :] + product_rows([fs_v], [res], base)

            loop_rows(node, 1, smooth_rows)
    x_out[...] = x_v[...]

    loads[4].wait()

    def pull_rows(i, total):
        for a in range(SUB):
            total = total + pr_v[i * SUB + a] * ax_v[pl.ds(i * SUB + a, 1), :]
        return total

    pulled = lax.fori_loop(0, node // SUB, pull_rows, jnp.zeros((node, LANES), jnp.float32))
    first = pulled.astype(jnp.bfloat16)
    rest = pulled - first.astype(jnp.float32)
    second = rest.astype(jnp.bfloat16)
    third = (rest - second.astype(jnp.float32)).astype(jnp.bfloat16)
    pieces = jnp.concatenate([first, second, third], axis=0)

    def restrict(q, carry):
        base = pl.multiple_of(q * LANES, LANES)
        table = lax.dot_general(
            pieces, onehot[pl.ds(base, LANES), :], (((1,), (1,)), ((), ())), preferred_element_type=jnp.float32
        )
        table = table[:node] + (table[node : 2 * node] + table[2 * node :])
        for j in range(groups):
            part_send[q * groups + j] = pack_rows(table, j * width + lane_mod)
        return carry

    lax.fori_loop(0, n_fine // groups, restrict, 0)

    def part_copy(t):
        return pltpu.make_async_remote_copy(
            part_send.at[t], part_recv.at[t], part_ssem, part_rsem, device_id=peer(t), device_id_type=MESH
        )

    def part_start(t, carry):
        part_copy(t).start()
        return carry

    lax.fori_loop(1, n_fine, part_start, 0)
    others = pl.ds(1, n_fine - 1)
    part_all = pltpu.make_async_remote_copy(
        part_send.at[others], part_recv.at[others], part_ssem, part_rsem, device_id=peer(1), device_id_type=MESH
    )
    part_all.wait_recv()
    owned = part_send[0]
    owned = lax.fori_loop(1, n_fine, lambda t, total: total + part_recv[t], owned)

    def expand(values):
        return jnp.concatenate(
            [
                lane_gather(values[h : h + SUB], g * width + lane_mod)
                for g in range(groups)
                for h in range(0, tall, SUB)
            ],
            axis=0,
        )

    right4 = expand(owned)

    def smoothed(vector):
        return jnp.concatenate(
            [product_rows([packed_sm], [vector], h) for h in range(0, tall, SUB)], axis=0
        )

    y = smoothed(right4)
    for s in range(COARSE_SWEEPS - 1):
        gathered[s, 0] = y

        def y_copy(t):
            return pltpu.make_async_remote_copy(
                gathered.at[s, 0], gathered.at[s, t], y_ssem.at[s], y_rsem.at[s], device_id=peer(t), device_id_type=MESH
            )

        def y_start(t, carry):
            y_copy(t).start()
            return carry

        lax.fori_loop(1, n_fine, y_start, 0)
        pltpu.make_async_remote_copy(
            gathered.at[s, others], gathered.at[s, others], y_ssem.at[s], y_rsem.at[s],
            device_id=peer(1), device_id_type=MESH,
        ).wait_recv()

        def pick(t, rows):
            mine = wanted_slot == t
            block = gathered[s, t]
            out = []
            for v in range(node // SUB):
                g, h = v * SUB // tall, v * SUB % tall
                piece = lane_gather(block[h : h + SUB], wanted_lane + g * width)
                out.append(jnp.where(mine, piece, rows[v]))
            return tuple(out)

        rows = lax.fori_loop(0, n_fine, pick, tuple(jnp.zeros((SUB, LANES), jnp.float32) for _ in range(node // SUB)))
        vector = jnp.concatenate(rows, axis=0)

        def op_rows(base):
            image = product_rows([packed_op], [vector], base)
            image = image + pltpu.roll(image, 2 * width, 1)
            gather4[pl.ds(base, SUB), :] = image + pltpu.roll(image, width, 1)

        loop_rows(node, 1, op_rows)
        y = y + smoothed(right4 - gather4[...])

    y_out[...] = expand(y)[:, :width]

    for s in range(FINE_SWEEPS):
        @pl.when(has_upper)
        def _():
            up_copy(s).wait_send()

        @pl.when(has_lower)
        def _():
            down_copy(s).wait_send()
    part_all.wait_send()
    for s in range(COARSE_SWEEPS - 1):
        pltpu.make_async_remote_copy(
            gathered.at[s, others], gathered.at[s, others], y_ssem.at[s], y_rsem.at[s],
            device_id=peer(1), device_id_type=MESH,
        ).wait_send()


def body(n_coarse, n_fine, rs, fd, fs, fc, fcol, su, sd, pr, ag, cd, cs, cc, ccol):
    node, blocks = rs.shape
    width = cd.shape[2]
    cd, cs, cc = (jnp.swapaxes(array, -1, -2) for array in (cd, cs, cc))
    groups = LANES // width
    tall = node // groups
    f32 = jnp.float32
    hbm = pl.BlockSpec(memory_space=pl.ANY)
    vmem = pl.BlockSpec(memory_space=pltpu.VMEM)
    sweeps, rounds = FINE_SWEEPS, COARSE_SWEEPS - 1
    return pl.pallas_call(
        functools.partial(kernel, n_coarse, n_fine),
        out_shape=(jax.ShapeDtypeStruct((node, blocks), f32), jax.ShapeDtypeStruct((node, width), f32)),
        in_specs=[hbm, hbm, hbm, hbm, vmem, vmem, vmem, hbm, vmem, hbm, hbm, hbm, vmem],
        out_specs=(vmem, vmem),
        scratch_shapes=[
            pltpu.VMEM(rs.shape, f32),
            pltpu.VMEM(fd.shape, f32),
            pltpu.VMEM(fs.shape, f32),
            pltpu.VMEM(fc.shape, f32),
            pltpu.VMEM(pr.shape, f32),
            pltpu.VMEM(cd.shape, f32),
            pltpu.VMEM(cs.shape, f32),
            pltpu.VMEM(cc.shape, f32),
            pltpu.VMEM((node, node, LANES), f32),
            pltpu.VMEM((tall, node, LANES), f32),
            pltpu.VMEM((node, LANES), f32),
            pltpu.VMEM((node, LANES), f32),
            pltpu.VMEM((sweeps, tall, LANES), f32),
            pltpu.VMEM((sweeps, tall, LANES), f32),
            pltpu.VMEM((sweeps, tall, LANES), f32),
            pltpu.VMEM((sweeps, tall, LANES), f32),
            pltpu.VMEM((n_fine * width, LANES), jnp.bfloat16),
            pltpu.VMEM((node, LANES), f32),
            pltpu.VMEM((n_fine, tall, LANES), f32),
            pltpu.VMEM((n_fine, tall, LANES), f32),
            pltpu.VMEM((rounds, n_fine, tall, LANES), f32),
            pltpu.VMEM((node, LANES), f32),
            pltpu.VMEM(((groups + 1) * SUB, LANES), jnp.int32),
            pltpu.SemaphoreType.DMA((8,)),
            pltpu.SemaphoreType.DMA((2, sweeps)),
            pltpu.SemaphoreType.DMA((2, sweeps)),
            pltpu.SemaphoreType.DMA,
            pltpu.SemaphoreType.DMA,
            pltpu.SemaphoreType.DMA((rounds,)),
            pltpu.SemaphoreType.DMA((rounds,)),
        ],
        compiler_params=pltpu.CompilerParams(
            collective_id=0, has_side_effects=True, vmem_limit_bytes=60 * 1024 * 1024
        ),
    )(rs, fd, fs, fc, fcol, su.reshape(1, -1), sd.reshape(1, -1), pr, ag.reshape(1, -1), cd, cs, cc, ccol)


def solution(mesh):
    blocks = ("coarse", "fine")
    in_specs = (
        P(None, blocks),
        P(None, None, blocks),
        P(None, None, blocks),
        P(None, None, None, blocks),
        P(None, blocks),
        P(blocks),
        P(blocks),
        P(None, None, blocks),
        P(blocks),
        P(None, None, blocks),
        P(None, None, blocks),
        P(None, None, None, blocks),
        P(None, blocks),
    )
    return jax.shard_map(
        functools.partial(body, mesh.shape["coarse"], mesh.shape["fine"]),
        mesh=mesh, in_specs=in_specs, out_specs=(P(None, blocks), P(None, blocks)), check_vma=False,
    )
```

time: 184 us -> 47.1 us (0.26)
  Pallas kernels: 0 us -> 43.4 us
  waiting for transfers between devices: 41.4 us -> 0 us
  blocking collectives: 35.3 us -> 0 us
  matrix products: 30.6 us -> 0 us
  local copies, waits for them, and re-layouts: 28.3 us -> 2.81 us
  other arithmetic: 17.4 us -> 0 us
  starting transfers between devices: 15.8 us -> 0 us
  between operations: 14.5 us -> 0.64 us
    pallas_call x0 -> x1, Pallas kernels: none -> 43.4 us  [body(): pl.pallas_call(functools.partial(kernel, n_coarse, n_fine), out_shape=(ja...]
    reduce_scatter x1 -> x0, waiting for transfers between devices: 40.4 us -> none  [body(): lax.psum_scatter(jnp.dot(pulled, onehot, precision=lax.Precision.HIGHEST)...]
    all_gather x4 -> x0, blocking collectives: 35.3 us -> none  [body(): gathered = lax.all_gather(correction, 'fine', axis=1, tiled=True)]
    dot_general x22 -> x0, matrix products: 30.6 us -> none  [the longest x21 29.6 us: apply_blocks(): jnp.einsum('abn,bn->an', blocks, vector, precision=lax.Precision.HIGHEST)]
    ppermute x6 -> x0, starting transfers between devices: 15.7 us -> none  [from_behind(): lax.ppermute(value, axis, [(source, source + steps) for source in range(l...]
    gather x24 -> x0, local copies, waits for them, and re-layouts: 14.2 us -> none  [the longest x12 6.87 us: body(): gathered[:, coarse_columns[neighbour]]]
    dot_general x7 -> x0, other arithmetic: 13.8 us -> none  [the longest x6 13.6 us: apply_blocks(): jnp.einsum('abn,bn->an', blocks, vector, precision=lax.Precision.HIGHEST)]
    squeeze x4 -> x0, local copies, waits for them, and re-layouts: 8.77 us -> none  [body(): coarse_coupling[neighbour]]
  transfers between devices with their start and end apart: 7 -> 0, of which waited for: 2 -> 0; matrix products, arithmetic and copies ran while one was open for 10% -> 0% of each run, Pallas kernels for 0% -> 0%
where the time goes in v1:
time: 47.1 us; the launch traced here: 46.8 us
  Pallas kernels  43.4 us (92%)
  local copies, waits for them, and re-layouts  2.81 us (6%)
  between operations  0.64 us (1%)
    pallas_call x1, Pallas kernels, body(): pl.pallas_call(functools.partial(kernel, n_coarse, n_fine), out_shape=(ja...  43.4 us
    pallas_call x1, local copies, waits for them, and re-layouts, body(): pl.pallas_call(functools.partial(kernel, n_coarse, n_fine), out_shape=(ja...  1.44 us
    unnamed x1, local copies, waits for them, and re-layouts  1.37 us

profile of v1, /device:TPU:0, one launch (start us, length us, event | category | flops | bytes accessed | tf_op | source)
XLA Modules:
  0.0 46.8 jit_solution(5545759866233458414)
XLA Ops:
  0.6 43.4 %shard_map.140 = (f32[64,128]{1,0:T(8,128)}, f32[64,32]{1,0:T(8,128)}) custom-call(f32[64,128]{1,0:T(8,128)} %rs.1, f32[64,64,128]{2,1,0:T(8,128)} %fd.1, f32[64,64,128]{2,1,0:T(8,128)} %fs.1, f32[2,64,64,128]{3,2,1,0:T(8,128)} %fc.1, s32[2,128]{1,0:T(2,128)} %fcol.1, s32[1,32]{1,0:T(1,128)} %bitcast.9, s32[1,32]{1,0:T(1,128)} %bitcast.10, ...), custom_call_target="tpu_custom_call" | custom-call | tf_op jit(solution)/shard_map/pallas_call | solution.py:385
  44.0 1.4 %copy.15 = f32[64,32]{0,1:T(8,128)} copy(f32[64,32]{1,0:T(8,128)} %get-tuple-element.3) | data formatting | bytes 16384 | tf_op jit(solution)/shard_map/pallas_call | solution.py:385
  45.5 1.4 %copy.17 = f32[64,128]{1,0:T(8,128)} copy(f32[64,128]{1,0:T(8,128)} %get-tuple-element.6) | data formatting | bytes 65536

commit v2 on v1

--- a/solution.py
+++ b/solution.py
@@ -12,6 +12,9 @@
 MESH = pl.DeviceIdType.MESH
 LANES = 128
 SUB = 8
+UNROLL = 8
+OP_SHARES = (0, 10, 23, 36, 50, 64)
+SM_SHARES = (0, 6, 11, 16, 16, 16)
 
 
 def lane_gather(values, index):
@@ -66,7 +69,7 @@
     tall = node // groups
     loads = []
     for slot, (src, dst) in enumerate(
-        [(rs, rs_v), (fs, fs_v), (fd, fd_v), (fc, fc_v), (pr, pr_v), (cc, cc_v), (cd, cd_v), (cs, cs_v)]
+        [(rs, rs_v), (fs, fs_v), (fd, fd_v), (fc, fc_v), (cc, cc_v), (cd, cd_v), (cs, cs_v), (pr, pr_v)]
     ):
         load = pltpu.make_async_copy(src, dst, load_sem.at[slot])
         load.start()
@@ -77,16 +80,19 @@
     down_id = (jnp.where(f > 0, c, c - 1), jnp.where(f > 0, f - 1, n_fine - 1))
     up_id = (jnp.where(f < n_fine - 1, c, c + 1), jnp.where(f < n_fine - 1, f + 1, 0))
 
-    def peer(t):
-        return (c, lax.rem(f + t, n_fine))
-
+    def peer(m):
+        place = f
+        for bit in range(n_fine.bit_length() - 1):
+            if m >> bit & 1:
+                place = place + (1 - 2 * lax.rem(f // 2**bit, 2)) * 2**bit
+        return (c, place)
+
+    far_first = range(n_fine - 1, 0, -1)
+    peers = [peer(m) for m in range(n_fine)]
     barrier = pltpu.get_barrier_semaphore()
 
-    def greet(t, carry):
-        pl.semaphore_signal(barrier, inc=1, device_id=peer(t), device_id_type=MESH)
-        return carry
-
-    lax.fori_loop(1, n_fine, greet, 0)
+    for m in far_first:
+        pl.semaphore_signal(barrier, inc=1, device_id=peers[m], device_id_type=MESH)
     cross_down = jnp.logical_and(f == 0, c > 0)
     cross_up = jnp.logical_and(f == n_fine - 1, c < n_coarse - 1)
 
@@ -117,11 +123,11 @@
     wanted = f * width + lane_mod
     for k in range(groups - 1):
         wanted = jnp.where(lane_group == k, spread(2 + k), wanted)
-    wanted_slot = lax.rem(f - wanted // width + n_fine, n_fine)
+    wanted_slot = jnp.bitwise_xor(wanted // width, f)
     wanted_lane = lax.rem(wanted, width)
 
     agg = ag[...]
-    agg_slot = lax.rem(agg // width - f + n_fine, n_fine) * width + lax.rem(agg, width)
+    agg_slot = jnp.bitwise_xor(agg // width, f) * width + lax.rem(agg, width)
 
     def hot_rows(t, carry):
         base = pl.multiple_of(t * width, width)
@@ -146,7 +152,7 @@
     def first_rows(base):
         x_v[pl.ds(base, SUB), :] = product_rows([fs_v], [right], base)
 
-    loop_rows(node, 1, first_rows)
+    loop_rows(node, UNROLL, first_rows)
 
     pl.semaphore_wait(barrier, n_fine - 1 + cross_down.astype(jnp.int32) + cross_up.astype(jnp.int32))
 
@@ -177,7 +183,10 @@
     is_low = [col < rim for col in columns]
     is_high = [col >= rim + LANES for col in columns]
 
-    def pack_coarse(part, parts):
+    def pack_coarse(part):
+        def loop(first, last, step):
+            lax.fori_loop(first, last, step, 0, unroll=last - first)
+
         def op_row(a, carry):
             packed_op[a] = jnp.concatenate([cc_v[k, a] for k in range(groups - 1)] + [cd_v[a]], axis=0).T
             return carry
@@ -186,18 +195,18 @@
             packed_sm[a] = jnp.concatenate([cs_v[g * tall + a] for g in range(groups)], axis=0).T
             return carry
 
-        lax.fori_loop(part * node // parts, (part + 1) * node // parts, op_row, 0)
-        lax.fori_loop(part * tall // parts, (part + 1) * tall // parts, sm_row, 0)
-
-    parts = 2
+        loop(OP_SHARES[part], OP_SHARES[part + 1], op_row)
+        loop(SM_SHARES[part], SM_SHARES[part + 1], sm_row)
+
     for s in range(FINE_SWEEPS):
         x = x_v[...]
         send_up[s] = pack_rows(x, up_index)
+
+        @pl.when(has_upper)
+        def _():
+            up_copy(s).start()
+
         send_down[s] = pack_rows(x, down_index)
-
-        @pl.when(has_upper)
-        def _():
-            up_copy(s).start()
 
         @pl.when(has_lower)
         def _():
@@ -209,14 +218,12 @@
         def diag_rows(base):
             ax_v[pl.ds(base, SUB), :] = product_rows([fd_v], [x], base)
 
-        loop_rows(node, 1, diag_rows)
+        loop_rows(node, UNROLL, diag_rows)
         if s == 0:
             loads[3].wait()
-        if s == 1:
-            for load in loads[5:]:
+            for load in loads[4:7]:
                 load.wait()
-        if s >= 1:
-            pack_coarse(s - 1, parts)
+        pack_coarse(s)
 
         @pl.when(has_lower)
         def _():
@@ -242,7 +249,7 @@
             image = product_rows([fc_v.at[k] for k in range(len(columns))], picked, base)
             ax_v[at, :] = rs_v[at, :] - (ax_v[at, :] + image)
 
-        loop_rows(node, 1, coupling_rows)
+        loop_rows(node, UNROLL, coupling_rows)
         if s < FINE_SWEEPS - 1:
             res = ax_v[...]
 
@@ -250,10 +257,10 @@
                 at = pl.ds(base, SUB)
                 x_v[at, :] = x_v[at, :] + product_rows([fs_v], [res], base)
 
-            loop_rows(node, 1, smooth_rows)
+            loop_rows(node, UNROLL, smooth_rows)
     x_out[...] = x_v[...]
 
-    loads[4].wait()
+    loads[7].wait()
 
     def pull_rows(i, total):
         for a in range(SUB):
@@ -267,35 +274,28 @@
     third = (rest - second.astype(jnp.float32)).astype(jnp.bfloat16)
     pieces = jnp.concatenate([first, second, third], axis=0)
 
-    def restrict(q, carry):
-        base = pl.multiple_of(q * LANES, LANES)
+    def part_copy(m):
+        return pltpu.make_async_remote_copy(
+            part_send.at[m], part_recv.at[m], part_ssem, part_rsem.at[m], device_id=peers[m], device_id_type=MESH
+        )
+
+    for q in reversed(range(n_fine // groups)):
         table = lax.dot_general(
-            pieces, onehot[pl.ds(base, LANES), :], (((1,), (1,)), ((), ())), preferred_element_type=jnp.float32
+            pieces, onehot[q * LANES : (q + 1) * LANES, :], (((1,), (1,)), ((), ())),
+            preferred_element_type=jnp.float32,
         )
         table = table[:node] + (table[node : 2 * node] + table[2 * node :])
-        for j in range(groups):
-            part_send[q * groups + j] = pack_rows(table, j * width + lane_mod)
-        return carry
-
-    lax.fori_loop(0, n_fine // groups, restrict, 0)
-
-    def part_copy(t):
-        return pltpu.make_async_remote_copy(
-            part_send.at[t], part_recv.at[t], part_ssem, part_rsem, device_id=peer(t), device_id_type=MESH
-        )
-
-    def part_start(t, carry):
-        part_copy(t).start()
-        return carry
-
-    lax.fori_loop(1, n_fine, part_start, 0)
+        for j in reversed(range(groups)):
+            m = q * groups + j
+            part_send[m] = pack_rows(table, j * width + lane_mod)
+            if m > 0:
+                part_copy(m).start()
+    pack_coarse(FINE_SWEEPS)
     others = pl.ds(1, n_fine - 1)
-    part_all = pltpu.make_async_remote_copy(
-        part_send.at[others], part_recv.at[others], part_ssem, part_rsem, device_id=peer(1), device_id_type=MESH
-    )
-    part_all.wait_recv()
     owned = part_send[0]
-    owned = lax.fori_loop(1, n_fine, lambda t, total: total + part_recv[t], owned)
+    for m in range(1, n_fine):
+        part_copy(m).wait_recv()
+        owned = owned + part_recv[m]
 
     def expand(values):
         return jnp.concatenate(
@@ -318,32 +318,25 @@
     for s in range(COARSE_SWEEPS - 1):
         gathered[s, 0] = y
 
-        def y_copy(t):
+        def y_copy(m):
             return pltpu.make_async_remote_copy(
-                gathered.at[s, 0], gathered.at[s, t], y_ssem.at[s], y_rsem.at[s], device_id=peer(t), device_id_type=MESH
+                gathered.at[s, 0], gathered.at[s, m], y_ssem.at[s], y_rsem.at[s, m],
+                device_id=peers[m], device_id_type=MESH,
             )
 
-        def y_start(t, carry):
-            y_copy(t).start()
-            return carry
-
-        lax.fori_loop(1, n_fine, y_start, 0)
-        pltpu.make_async_remote_copy(
-            gathered.at[s, others], gathered.at[s, others], y_ssem.at[s], y_rsem.at[s],
-            device_id=peer(1), device_id_type=MESH,
-        ).wait_recv()
-
-        def pick(t, rows):
-            mine = wanted_slot == t
-            block = gathered[s, t]
-            out = []
+        for m in far_first:
+            y_copy(m).start()
+        if s == 0:
+            pack_coarse(FINE_SWEEPS + 1)
+        rows = [None] * (node // SUB)
+        for m in range(n_fine):
+            if m > 0:
+                y_copy(m).wait_recv()
+            mine = wanted_slot == m
             for v in range(node // SUB):
                 g, h = v * SUB // tall, v * SUB % tall
-                piece = lane_gather(block[h : h + SUB], wanted_lane + g * width)
-                out.append(jnp.where(mine, piece, rows[v]))
-            return tuple(out)
-
-        rows = lax.fori_loop(0, n_fine, pick, tuple(jnp.zeros((SUB, LANES), jnp.float32) for _ in range(node // SUB)))
+                piece = lane_gather(gathered[s, m, h : h + SUB], wanted_lane + g * width)
+                rows[v] = piece if m == 0 else jnp.where(mine, piece, rows[v])
         vector = jnp.concatenate(rows, axis=0)
 
         def op_rows(base):
@@ -351,10 +344,10 @@
             image = image + pltpu.roll(image, 2 * width, 1)
             gather4[pl.ds(base, SUB), :] = image + pltpu.roll(image, width, 1)
 
-        loop_rows(node, 1, op_rows)
+        loop_rows(node, UNROLL, op_rows)
         y = y + smoothed(right4 - gather4[...])
 
-    y_out[...] = expand(y)[:, :width]
+    y_out[...] = expand(y).T[:width]
 
     for s in range(FINE_SWEEPS):
         @pl.when(has_upper)
@@ -364,11 +357,13 @@
         @pl.when(has_lower)
         def _():
             down_copy(s).wait_send()
-    part_all.wait_send()
+    pltpu.make_async_remote_copy(
+        part_send.at[others], part_recv.at[others], part_ssem, part_rsem.at[1], device_id=peers[1], device_id_type=MESH
+    ).wait_send()
     for s in range(COARSE_SWEEPS - 1):
         pltpu.make_async_remote_copy(
-            gathered.at[s, others], gathered.at[s, others], y_ssem.at[s], y_rsem.at[s],
-            device_id=peer(1), device_id_type=MESH,
+            gathered.at[s, others], gathered.at[s, others], y_ssem.at[s], y_rsem.at[s, 1],
+            device_id=peers[1], device_id_type=MESH,
         ).wait_send()
 
 
@@ -382,9 +377,9 @@
     hbm = pl.BlockSpec(memory_space=pl.ANY)
     vmem = pl.BlockSpec(memory_space=pltpu.VMEM)
     sweeps, rounds = FINE_SWEEPS, COARSE_SWEEPS - 1
-    return pl.pallas_call(
+    x, y = pl.pallas_call(
         functools.partial(kernel, n_coarse, n_fine),
-        out_shape=(jax.ShapeDtypeStruct((node, blocks), f32), jax.ShapeDtypeStruct((node, width), f32)),
+        out_shape=(jax.ShapeDtypeStruct((node, blocks), f32), jax.ShapeDtypeStruct((width, node), f32)),
         in_specs=[hbm, hbm, hbm, hbm, vmem, vmem, vmem, hbm, vmem, hbm, hbm, hbm, vmem],
         out_specs=(vmem, vmem),
         scratch_shapes=[
@@ -415,14 +410,15 @@
             pltpu.SemaphoreType.DMA((2, sweeps)),
             pltpu.SemaphoreType.DMA((2, sweeps)),
             pltpu.SemaphoreType.DMA,
-            pltpu.SemaphoreType.DMA,
+            pltpu.SemaphoreType.DMA((n_fine,)),
             pltpu.SemaphoreType.DMA((rounds,)),
-            pltpu.SemaphoreType.DMA((rounds,)),
+            pltpu.SemaphoreType.DMA((rounds, n_fine)),
         ],
         compiler_params=pltpu.CompilerParams(
             collective_id=0, has_side_effects=True, vmem_limit_bytes=60 * 1024 * 1024
         ),
     )(rs, fd, fs, fc, fcol, su.reshape(1, -1), sd.reshape(1, -1), pr, ag.reshape(1, -1), cd, cs, cc, ccol)
+    return x, y.T
 
 
 def solution(mesh):

time: 47.1 us -> 39.6 us (0.84)
  Pallas kernels: 43.4 us -> 36 us
    pallas_call x1, Pallas kernels: 43.4 us -> 36 us  [body(): pl.pallas_call(functools.partial(kernel, n_coarse, n_fine), out_shape=(ja...]
    pallas_call x1 -> x0, local copies, waits for them, and re-layouts: 1.44 us -> none  [body(): pl.pallas_call(functools.partial(kernel, n_coarse, n_fine), out_shape=(ja...]
    unnamed x1 -> x2, local copies, waits for them, and re-layouts: 1.37 us -> 2.7 us
where the time goes in v2:
time: 39.6 us; the launch traced here: 39.3 us
  Pallas kernels  36 us (91%)
  local copies, waits for them, and re-layouts  2.7 us (7%)
  between operations  0.64 us (2%)
    pallas_call x1, Pallas kernels, body(): pl.pallas_call(functools.partial(kernel, n_coarse, n_fine), out_shape=(ja...  36 us
    unnamed x2, local copies, waits for them, and re-layouts  2.7 us

profile of v2, /device:TPU:0, one launch (start us, length us, event | category | flops | bytes accessed | tf_op | source)
XLA Modules:
  0.0 39.3 jit_solution(4496798527758698468)
XLA Ops:
  0.6 36.0 %shard_map.140 = (f32[64,128]{1,0:T(8,128)}, f32[32,64]{1,0:T(8,128)}) custom-call(f32[64,128]{1,0:T(8,128)} %rs.1, f32[64,64,128]{2,1,0:T(8,128)} %fd.1, f32[64,64,128]{2,1,0:T(8,128)} %fs.1, f32[2,64,64,128]{3,2,1,0:T(8,128)} %fc.1, s32[2,128]{1,0:T(2,128)} %fcol.1, s32[1,32]{1,0:T(1,128)} %bitcast.11, s32[1,32]{1,0:T(1,128)} %bitcast.12, ...), custom_call_target="tpu_custom_call" | custom-call | tf_op jit(solution)/shard_map/pallas_call | solution.py:380
  36.6 1.4 %copy.17 = f32[64,128]{1,0:T(8,128)} copy(f32[64,128]{1,0:T(8,128)} %get-tuple-element.8) | data formatting | bytes 65536
  38.0 1.3 %copy.18 = f32[64,32]{0,1:T(8,128)} copy(f32[64,32]{0,1:T(8,128)} %bitcast.10) | data formatting | bytes 16384

commit v3 on v2

--- a/solution.py
+++ b/solution.py
@@ -365,6 +365,11 @@
             gathered.at[s, others], gathered.at[s, others], y_ssem.at[s], y_rsem.at[s, 1],
             device_id=peers[1], device_id_type=MESH,
         ).wait_send()
+
+
+def place_results(x, y, x_out, y_out):
+    x_out[...] = x[...]
+    y_out[...] = y[...]
 
 
 def body(n_coarse, n_fine, rs, fd, fs, fc, fcol, su, sd, pr, ag, cd, cs, cc, ccol):
@@ -418,6 +423,12 @@
             collective_id=0, has_side_effects=True, vmem_limit_bytes=60 * 1024 * 1024
         ),
     )(rs, fd, fs, fc, fcol, su.reshape(1, -1), sd.reshape(1, -1), pr, ag.reshape(1, -1), cd, cs, cc, ccol)
+    x, y = pl.pallas_call(
+        place_results,
+        out_shape=(jax.ShapeDtypeStruct(x.shape, f32), jax.ShapeDtypeStruct(y.shape, f32)),
+        in_specs=[vmem, vmem],
+        out_specs=(vmem, vmem),
+    )(x, y)
     return x, y.T
 
 

time: 39.6 us -> 38.2 us (0.965)
  local copies, waits for them, and re-layouts: 2.7 us -> 0 us
  Pallas kernels: 36 us -> 37.3 us
    unnamed x2 -> x0, local copies, waits for them, and re-layouts: 2.7 us -> none
    pallas_call x0 -> x1, Pallas kernels: none -> 1.38 us  [body(): pl.pallas_call(place_results, out_shape=(jax.ShapeDtypeStruct(x.shape, f3...]
where the time goes in v3:
time: 38.2 us; the launch traced here: 38 us
  Pallas kernels  37.3 us (98%)
  between operations  0.64 us (2%)
    pallas_call x1, Pallas kernels, body(): pl.pallas_call(functools.partial(kernel, n_coarse, n_fine), out_shape=(ja...  35.9 us
    pallas_call x1, Pallas kernels, body(): pl.pallas_call(place_results, out_shape=(jax.ShapeDtypeStruct(x.shape, f3...  1.38 us

profile of v3, /device:TPU:0, one launch (start us, length us, event | category | flops | bytes accessed | tf_op | source)
XLA Modules:
  0.0 38.0 jit_solution(1773109937445255361)
XLA Ops:
  0.6 35.9 %shard_map.140 = (f32[64,128]{1,0:T(8,128)}, f32[32,64]{1,0:T(8,128)}) custom-call(f32[64,128]{1,0:T(8,128)} %rs.1, f32[64,64,128]{2,1,0:T(8,128)} %fd.1, f32[64,64,128]{2,1,0:T(8,128)} %fs.1, f32[2,64,64,128]{3,2,1,0:T(8,128)} %fc.1, s32[2,128]{1,0:T(2,128)} %fcol.1, s32[1,32]{1,0:T(1,128)} %bitcast.10, s32[1,32]{1,0:T(1,128)} %bitcast.11, ...), custom_call_target="tpu_custom_call" | custom-call | tf_op jit(solution)/shard_map/pallas_call | solution.py:385
  36.6 1.4 %shard_map.141 = (f32[64,128]{1,0:T(8,128)}, f32[32,64]{1,0:T(8,128)}) custom-call(f32[64,128]{1,0:T(8,128)} %get-tuple-element.6.x, f32[32,64]{1,0:T(8,128)} %get-tuple-element.7.y), custom_call_target="tpu_custom_call" | custom-call | tf_op jit(solution)/shard_map/pallas_call | solution.py:426
